TPU v7x, 32 devices: a whole 2x2x4 slice. The times are simulated.
32 devices in a mesh: dom: 2 (over core), rep: 16 (over z, y, x).
Axes of the slice: x: 2, y: 2, z: 4, core: 2. Of those that a mesh axis runs over, the one named last changes fastest.
Arguments:
- cells: int32 [3, 524288], P(None, ('dom', 'rep')), may hold values from 0 to 191, as said below
- offsets: float32 [3, 524288], P(None, ('dom', 'rep')), may hold values from 0 to 1
- displacements: float32 [3, 524288], P(None, ('dom', 'rep')), may hold values from -1 to 1
- block_split: int32 [16384], P(('dom', 'rep')), may hold values from 8 to 24
- fields: float32 [2, 4, 36864], P(None, 'dom'), may hold values from -12 to 12
- crossing: int32 [32, 2, 16], P(('dom', 'rep')), may hold values from 0 to 511, as said below
- crossing_counts: int32 [32, 2], P(('dom', 'rep')), may hold values from 0 to 16, as said below
Outputs:
- new_offsets: float32 [3, 524288], P(None, ('dom', 'rep'))
- density: float32 [2, 4, 36864], P(None, 'dom', 'rep')
- arrivals: float32 [2, 3, 16384], P(None, None, ('dom', 'rep'))
Inputs may be any that keep to these rules, and one draw needn't show every extreme that they name: x and y cells 0 to 191, z the layer 0 to 1 within the bead's domain; consecutive beads of a chain lie at most one cell apart along each direction (x and y periodically). `crossing`: the 32 entries of one device are distinct chain indices of that device. `crossing_counts`: the used slots are the first ones.
All inputs are finite; a program needn't handle non-finite values.
Results may differ from a plain program's by a relative error of at most 0.0003.
Values sent between devices are 32-bit elements; how exact they have to be, the bound alone decides.
A program may use at most 192 MiB of HBM per device.

v0:
```python
import jax
import jax.numpy as jnp
from jax import lax
from jax.sharding import PartitionSpec as P

GRID = 192


MOBILITY = 0.1


def shifted_2(value, axis, steps):
    count = lax.axis_size(axis)
    pairs = [(source, (source + steps) % count) for source in range(count)]
    return lax.ppermute(value, axis, pairs)


def padded_2(cells, sides, width):
    for axis, dim in sides:
        count = lax.axis_size(axis)
        head = lax.slice_in_dim(cells, 0, width, axis=dim)
        tail = lax.slice_in_dim(cells, cells.shape[dim] - width, cells.shape[dim], axis=dim)
        cells = jnp.concatenate(
            [
                lax.ppermute(tail, axis, [(i, (i + 1) % count) for i in range(count)]),
                cells,
                lax.ppermute(head, axis, [((i + 1) % count, i) for i in range(count)]),
            ],
            axis=dim,
        )
    return cells


def wrap_gap(stride_gap, period):
    return (stride_gap + period // 2) % period - period // 2


def bond_force(cell_rows, offset_rows):
    stride_gap = cell_rows[:, 1:] - cell_rows[:, :-1]
    plane_gap = wrap_gap(stride_gap[:2], GRID)
    stride_gap = jnp.concatenate([plane_gap, stride_gap[2:]], axis=0).astype(jnp.float32)
    stride_gap = stride_gap + (offset_rows[:, 1:] - offset_rows[:, :-1])
    zeros_row = jnp.zeros_like(stride_gap[:, :1])
    return jnp.concatenate([stride_gap, zeros_row], axis=1) - jnp.concatenate(
        [zeros_row, stride_gap], axis=1
    )


def field_forces(padded):
    interior = padded[:, 1:-1]
    layer_count = interior.shape[1]
    force_z = (padded[:, :-2] - padded[:, 2:]) * 0.5
    square = interior.reshape(2, layer_count, GRID, GRID)
    force_x = ((jnp.roll(square, 1, 2) - jnp.roll(square, -1, 2)) * 0.5).reshape(
        2, layer_count, GRID * GRID
    )
    force_y = ((jnp.roll(square, 1, 3) - jnp.roll(square, -1, 3)) * 0.5).reshape(
        2, layer_count, GRID * GRID
    )
    return jnp.stack([force_x, force_y, force_z]).reshape(3, -1)


def move_beads(cell_rows, offset_rows, displace_rows, split_rows, forces, layer_count):
    bead_count = cell_rows.shape[1]
    positions_along = jnp.arange(bead_count, dtype=jnp.int32)[:, None]
    species = (positions_along >= split_rows[None, :]).astype(jnp.int32)
    plane_index = cell_rows[0] * GRID + cell_rows[1]
    layer_of = cell_rows[2]
    lookup = species * (layer_count * GRID * GRID) + layer_of * (GRID * GRID) + plane_index
    field_push = forces[:, lookup]
    shifted = (
        offset_rows + MOBILITY * (bond_force(cell_rows, offset_rows) + field_push) + displace_rows
    )
    return (shifted, species, plane_index, layer_of)


def deposit(shifted, species, plane_index, layer_of, layer_count):
    upper_share = jnp.clip(shifted[2], 0.0, 1.0)
    base_index = species * (layer_count * GRID * GRID) + plane_index
    lower_index = (base_index + layer_of * (GRID * GRID)).reshape(-1)
    upper_index = (base_index + (layer_of + 1) * (GRID * GRID)).reshape(-1)
    all_index = jnp.concatenate([lower_index, upper_index])
    all_weight = jnp.concatenate([(1.0 - upper_share).reshape(-1), upper_share.reshape(-1)])
    grid_sum = jnp.zeros((2 * layer_count * GRID * GRID,), jnp.float32)
    return grid_sum.at[all_index].add(all_weight)


def crossing_rows(cell_rows, shifted, chosen, count_used, lift_by):
    position = cell_rows.astype(jnp.float32) + shifted
    picked = jnp.take(position, chosen, axis=2)
    picked = picked.at[2].add(lift_by)
    kept_mask = (jnp.arange(chosen.shape[0], dtype=jnp.int32) < count_used).astype(jnp.float32)
    return (picked * kept_mask).reshape(3, -1)


def send_up(rim_layer, rising):
    return shifted_2((rim_layer, rising), "dom", 1)


def reduce_grid(grid_sum):
    summed_all = lax.psum(grid_sum, "rep")
    share_width = grid_sum.shape[2] // lax.axis_size("rep")
    return lax.dynamic_slice_in_dim(summed_all, lax.axis_index("rep") * share_width, share_width, 2)


def shards(cells, offsets, displacements, block_split, fields, crossing, crossing_counts):
    chain_count = block_split.shape[0]
    bead_count = cells.shape[1] // chain_count
    layer_count = fields.shape[1]
    plane_size = GRID * GRID
    cell_rows = cells.reshape(3, bead_count, chain_count)
    offset_rows = offsets.reshape(3, bead_count, chain_count)
    displace_rows = displacements.reshape(3, bead_count, chain_count)
    padded = padded_2(fields, (("dom", 1),), 1)
    forces = field_forces(padded)
    shifted, species, plane_index, layer_of = move_beads(
        cell_rows, offset_rows, displace_rows, block_split, forces, layer_count
    )
    partial_grid = deposit(shifted, species, plane_index, layer_of, layer_count + 1).reshape(
        2, layer_count + 1, plane_size
    )
    rising = crossing_rows(
        cell_rows, shifted, crossing[0, 0], crossing_counts[0, 0], -float(layer_count)
    )
    falling = crossing_rows(
        cell_rows, shifted, crossing[0, 1], crossing_counts[0, 1], float(layer_count)
    )
    carried, arrived_up = send_up(partial_grid[:, layer_count:], rising)
    grid_sum = jnp.concatenate(
        [partial_grid[:, :1] + carried, partial_grid[:, 1:layer_count]], axis=1
    )
    density_sum = reduce_grid(grid_sum)
    arrived_down = shifted_2(falling, "dom", -1)
    density_scale = GRID * GRID * layer_count / (lax.axis_size("rep") * chain_count * bead_count)
    return (
        shifted.reshape(3, -1),
        density_sum * density_scale,
        jnp.stack([arrived_up, arrived_down]),
    )


def solution(mesh):
    in_specs = (
        P(None, ("dom", "rep")),
        P(None, ("dom", "rep")),
        P(None, ("dom", "rep")),
        P(("dom", "rep")),
        P(None, "dom", None),
        P(("dom", "rep"), None, None),
        P(("dom", "rep"), None),
    )
    out_specs = (P(None, ("dom", "rep")), P(None, "dom", "rep"), P(None, None, ("dom", "rep")))
    return jax.shard_map(shards, mesh=mesh, in_specs=in_specs, out_specs=out_specs, check_vma=False)
```

profile of v0, /device:TPU:15, one launch (start us, length us, event | category | flops | bytes accessed | tf_op | source)
XLA Modules:
  0.0 605.3 jit_solution(8908312575110286520)
XLA Ops:
  7.2 1.8 fusion.22
  9.1 0.9 copy.75
  10.0 0.7 collective-permute-start
  10.7 0.9 copy.76
  11.6 0.6 reshape.439
  12.2 0.3 fusion.20
  12.4 0.2 fusion.21
  12.8 0.6 copy-done.1
  13.4 1.6 slice_multiply_fusion
  15.1 0.7 fusion.9
  15.8 0.4 fusion.1
  16.2 0.7 mul.172
  17.2 1.6 mul.170
  18.7 0.9 mul.178
  19.6 0.9 fusion.11
  20.5 0.6 broadcast_clamp_fusion
  21.1 1.0 copy.101
  22.2 0.6 fusion.23
  22.8 1.1 compare_convert_fusion.1
  24.0 0.8 compare_select_fusion
  24.8 1.2 compare_convert_fusion
  26.0 0.7 fusion.6
  26.7 1.3 copy.62
  28.0 1.3 copy.64
  29.2 1.1 fusion.3
  30.3 0.9 stack.15
  31.2 2.8 pad_maximum_fusion
  34.1 34.2 %copy.65 = f32[3,147456]{0,1:T(8,128)} copy(f32[3,147456]{1,0:T(4,128)S(1)} %pad_maximum_fusion) | data formatting | bytes 3538944 | tf_op jit(solution)/shard_map/stack | solution.py:60
  68.3 237.6 %gather_fusion = f32[16384,3]{1,0:T(8,128)} fusion(f32[3,147456]{0,1:T(8,128)} %copy.65, s32[16384]{0:T(1024)S(1)} %copy-done.8), kind=kCustom, calls=%fused_computation.2 | custom fusion | bytes 458752 | tf_op jit(solution)/shard_map/gather | solution.py:70
  305.9 5.3 copy.74
  311.2 0.2 convert_add_fusion
  311.4 0.4 copy.67
  311.8 0.6 gather_fusion.1
  312.4 0.6 gather_fusion.2
  313.1 171.5 %scatter_custom_fusion = f32[221184]{0:T(1024)S(1)} fusion(s32[32768]{0:T(1024)} %bitcast.86, f32[32768]{0:T(1024)S(1)} %pad_maximum_fusion.4, f32[]{:T(128)} %constant.101.clone.1), kind=kCustom, calls=%fused_computation.15 | custom fusion | flops 32768 | bytes 885248 | tf_op jit(solution)/shard_map/scatter-add | solution.py:85
  484.5 0.4 reshape.442
  485.0 0.3 slice.197
  485.3 0.6 collective-permute-start.2
  486.0 1.1 collective-permute-done.2
  487.1 0.5 slice_add_fusion
  487.6 1.4 pad_maximum_fusion.3
  489.3 0.4 collective-permute-start.3
  490.0 0.2 collective-permute-start.4
  490.2 0.8 copy.81
  491.0 0.2 collective-permute-done.4
  491.2 0.6 copy.73
  491.8 105.2 %all-reduce.4.cloned.1.call-done = f32[2,2,36864]{2,1,0:T(2,128)} async-done(((f32[2,2,36864]{2,1,0:T(2,128)}), f32[2,2,36864]{2,1,0:T(2,128)}) %all-reduce.4.cloned.1.call-update) | async-done | bytes 589840 | tf_op jit(solution)/shard_map/psum | solution.py:101
  597.1 1.4 dynamic-slice_multiply_fusion
  (67 shorter events, 1.2 us)
Async XLA Ops:
  7.2 4.4 copy-start
  7.2 589.9 %all-reduce.4.cloned.1.call-start = ((), (), s32[]{:S(2)}) async-start(), calls=%async_computation | async-start | bytes 1179648 | tf_op jit(solution)/shard_map/psum | solution.py:101
  10.0 16.7 %collective-permute-start = (f32[2,1,36864]{2,0,1:T(2,128)}, f32[2,1,36864]{2,0,1:T(2,128)}, u32[]{:S(2)}, u32[]{:S(2)}) collective-permute-start(f32[2,1,36864]{2,0,1:T(2,128)} %copy.75), channel_id=1, source_target_pairs={{0,16},{16,0},{1,17},{17,1},{2,18},{18,2},{3,19},{19,3},{4,20},{20... | collective-permute-start | bytes 884744 | tf_op jit(solution)/shard_map/ppermute | solution.py:25
  11.6 16.4 %collective-permute-start.1 = (f32[2,1,36864]{2,0,1:T(2,128)}, f32[2,1,36864]{2,0,1:T(2,128)}, u32[]{:S(2)}, u32[]{:S(2)}) collective-permute-start(f32[2,1,36864]{2,0,1:T(2,128)} %copy.76), channel_id=1, source_target_pairs={{16,0},{0,16},{17,1},{1,17},{18,2},{2,18},{19,3},{3,19},{20,4},{4,... | collective-permute-start | bytes 884744 | tf_op jit(solution)/shard_map/ppermute | solution.py:27
  12.4 1.0 copy-start.1
  15.1 0.7 copy-start.5
  16.2 3.4 copy-start.12
  17.1 5.1 copy-start.14
  17.1 5.1 copy-start.13
  17.1 6.9 %copy-start.6 = (s32[1,16384]{1,0:T(1,128)S(1)}, s32[1,16384]{1,0:T(1,128)}, u32[]{:S(2)}) copy-start(s32[1,16384]{1,0:T(1,128)} %get-tuple-element.61) | copy-start | bytes 196612
  17.1 6.9 %copy-start.9 = (s32[1,16384]{1,0:T(1,128)S(1)}, s32[1,16384]{1,0:T(1,128)}, u32[]{:S(2)}) copy-start(s32[1,16384]{1,0:T(1,128)} %get-tuple-element.58) | copy-start | bytes 196612
  17.1 6.9 %copy-start.10 = (s32[1,16384]{1,0:T(1,128)S(1)}, s32[1,16384]{1,0:T(1,128)}, u32[]{:S(2)}) copy-start(s32[1,16384]{1,0:T(1,128)} %get-tuple-element.60) | copy-start | bytes 196612
  17.1 8.8 %slice-start = ((s32[3,31,512]{2,1,0:T(8,128)}), s32[1,31,512]{2,1,0:T(8,128)S(1)}, s32[]{:S(2)}) async-start(s32[3,31,512]{2,1,0:T(8,128)} %copy-done.5), calls=%async_computation.1 | async-start | bytes 131072 | tf_op jit(solution)/shard_map/slice | solution.py:41
  17.1 8.8 %copy-start.7 = (s32[2,31,512]{2,1,0:T(8,128)S(1)}, s32[2,31,512]{2,1,0:T(8,128)}, u32[]{:S(2)}) copy-start(s32[2,31,512]{2,1,0:T(8,128)} %fusion.9) | copy-start | bytes 380932
  34.1 34.2 %copy-start.8 = (s32[16384]{0:T(1024)S(1)}, s32[16384]{0:T(1024)}, u32[]{:S(2)}) copy-start(s32[16384]{0:T(1024)} %broadcast_clamp_fusion) | copy-start | bytes 196612
  305.8 5.3 copy-start.2
  305.8 5.3 copy-start.3
  305.8 5.4 copy-start.4
  305.8 5.4 copy-start.11
  485.0 4.0 copy-start.15
  485.0 4.7 copy-start.16
  485.3 1.8 collective-permute-start.2
  489.3 1.7 collective-permute-start.3
  490.0 1.2 collective-permute-start.4
Sparse Core Ops, SparseCore 0:
  489.1 107.8 all-reduce.3
where the time goes:
time: 612 us; the launch traced here: 605 us
  local copies, waits for them, and re-layouts  295 us (48%)
  other arithmetic  187 us (31%)
  waiting for transfers between devices  107 us (17%)
  between operations  14.5 us (2%)
    gather x2, local copies, waits for them, and re-layouts, move_beads(): field_push = forces[:, lookup]  243 us
    scatter-add x1, other arithmetic, deposit(): return grid_sum.at[all_index].add(all_weight)  171 us
    psum x1, waiting for transfers between devices, reduce_grid(): summed_all = lax.psum(grid_sum, 'rep')  105 us
    another operation x2, local copies, waits for them, and re-layouts, field_forces(): return jnp.stack([force_x, force_y, force_z]).reshape(3, -1)  35.1 us
  transfers between devices with their start and end apart: 6, of which 3 were waited for; matrix products, arithmetic and copies ran while one was open for 3% of the time, Pallas kernels for 0%

commit v1 on v0

v1 whole, which is shorter than its diff:
```python
import functools

import jax
import jax.numpy as jnp
from jax import lax
from jax.experimental import pallas as pl
from jax.experimental.pallas import tpu as pltpu
from jax.sharding import PartitionSpec as P

GRID = 192


MOBILITY = 0.1


def step_kernel(
    layers, beads, chains, slots, group, scale,
    count_ref, cells_ref, offsets_ref, displace_ref, split_ref, field_ref, low_ref, high_ref,
    cross_ref, out_ref, grid_ref, carry_ref, picked_ref,
    table_hi, table_lo, hot, weights, total, position,
):
    planes = 2 * layers
    keys = planes * GRID

    for s in range(2):
        for layer in range(layers):
            q = s * layers + layer
            w = field_ref[q]
            below = low_ref[s] if layer == 0 else field_ref[q - 1]
            above = high_ref[s] if layer == layers - 1 else field_ref[q + 1]
            back_x = jnp.concatenate([w[GRID - 1 :], w[: GRID - 1]], axis=0)
            ahead_x = jnp.concatenate([w[1:], w[:1]], axis=0)
            back_y = jnp.concatenate([w[:, GRID - 1 :], w[:, : GRID - 1]], axis=1)
            ahead_y = jnp.concatenate([w[:, 1:], w[:, :1]], axis=1)
            forces = (back_x - ahead_x, back_y - ahead_y, below - above)
            for k, force in enumerate(forces):
                force = force * 0.5
                top = force.astype(jnp.bfloat16)
                rest = (force - top.astype(jnp.float32)).astype(jnp.bfloat16)
                table_hi[k * GRID : (k + 1) * GRID, q * GRID : (q + 1) * GRID] = top
                table_lo[k * GRID : (k + 1) * GRID, q * GRID : (q + 1) * GRID] = rest

    total[...] = jnp.zeros_like(total)
    key_rows = lax.broadcasted_iota(jnp.int32, (keys, chains), 0)
    x_rows = lax.broadcasted_iota(jnp.int32, (GRID, chains), 0)

    def gap(cell_a, off_a, cell_b, off_b):
        d = cell_b - cell_a
        d = jnp.where(d > GRID // 2 - 1, d - GRID, jnp.where(d < -(GRID // 2), d + GRID, d))
        return d.astype(jnp.float32) + (off_b - off_a)

    def columns(j):
        return pl.ds(pl.multiple_of(j * chains, 128), chains)

    @pl.loop(0, beads // group)
    def _(g):
        for jj in range(group):
            j = g * group + jj
            here = columns(j)
            after = columns(jnp.minimum(j + 1, beads - 1))
            before = columns(jnp.maximum(j - 1, 0))
            cell, off = cells_ref[:, here], offsets_ref[:, here]
            gap_after = gap(cell, off, cells_ref[:, after], offsets_ref[:, after])
            gap_before = gap(cells_ref[:, before], offsets_ref[:, before], cell, off)
            bond = gap_after - gap_before
            species = (split_ref[...] <= j).astype(jnp.int32)
            key = (species * layers + cell[2:3]) * GRID + cell[1:2]
            chosen = jnp.where(key_rows == key, 1.0, 0.0).astype(jnp.bfloat16)
            hot[:, jj * chains : (jj + 1) * chains] = chosen
            found = jnp.dot(table_hi[...], chosen, preferred_element_type=jnp.float32)
            found += jnp.dot(table_lo[...], chosen, preferred_element_type=jnp.float32)
            at_x = x_rows == cell[0:1]
            push = [
                jnp.sum(
                    jnp.where(at_x, found[k * GRID : (k + 1) * GRID], 0.0), axis=0, keepdims=True
                )
                for k in range(3)
            ]
            moved = off + MOBILITY * (bond + jnp.concatenate(push, axis=0)) + displace_ref[:, here]
            out_ref[:, here] = moved
            place = cell.astype(jnp.float32) + moved
            for k in range(3):
                position[pl.ds(k * beads + j, 1), :] = place[k : k + 1]
            t = jnp.clip(moved[2:3], 0.0, 1.0)
            top = t.astype(jnp.bfloat16).astype(jnp.float32)
            here_w = slice(jj * chains, (jj + 1) * chains)
            weights[0:GRID, here_w] = jnp.where(at_x, 1.0, 0.0).astype(jnp.bfloat16)
            weights[GRID : 2 * GRID, here_w] = jnp.where(at_x, top, 0.0).astype(jnp.bfloat16)
            weights[2 * GRID :, here_w] = jnp.where(at_x, t - top, 0.0).astype(jnp.bfloat16)
        total[...] += lax.dot_general(
            weights[...], hot[...], (((1,), (1,)), ((), ())), preferred_element_type=jnp.float32
        )

    ones = total[0:GRID]
    upper = total[GRID : 2 * GRID] + total[2 * GRID :]
    lower = (ones - upper) * scale
    upper = upper * scale
    for s in range(2):
        for layer in range(layers):
            q = s * layers + layer
            part = lower[:, q * GRID : (q + 1) * GRID]
            if layer > 0:
                part = part + upper[:, (q - 1) * GRID : q * GRID]
            grid_ref[q] = part
        last = s * layers + layers - 1
        carry_ref[s] = upper[:, last * GRID : (last + 1) * GRID]

    chain_rows = lax.broadcasted_iota(jnp.int32, (chains, 2 * slots), 0)
    pick = jnp.where(chain_rows == cross_ref[...], 1.0, 0.0)
    picked = jnp.dot(
        position[...], pick, precision=lax.Precision.HIGHEST, preferred_element_type=jnp.float32
    )
    rows = lax.broadcasted_iota(jnp.int32, picked.shape, 0)
    slot = lax.broadcasted_iota(jnp.int32, picked.shape, 1)
    upward = slot < slots
    lift = jnp.where(upward, -float(layers), float(layers))
    picked = jnp.where(rows >= 2 * beads, picked + lift, picked)
    limit = jnp.where(upward, count_ref[0, 0], slots + count_ref[0, 1])
    picked_ref[...] = jnp.where(slot < limit, picked, 0.0)


def shifted(value, axis, steps):
    count = lax.axis_size(axis)
    return lax.ppermute(value, axis, [(i, (i + steps) % count) for i in range(count)])


def shards(cells, offsets, displacements, block_split, fields, crossing, crossing_counts):
    chains = block_split.shape[0]
    beads = cells.shape[1] // chains
    layers = fields.shape[1]
    slots = crossing.shape[2]
    plane = GRID * GRID
    group = 4
    scale = plane * layers / (lax.axis_size("rep") * chains * beads)
    square = fields.reshape(2, layers, GRID, GRID)
    low = shifted(square[:, layers - 1], "dom", 1)
    high = shifted(square[:, 0], "dom", -1)
    vmem = pl.BlockSpec(memory_space=pltpu.VMEM)
    new_offsets, grid, carry, picked = pl.pallas_call(
        functools.partial(step_kernel, layers, beads, chains, slots, group, scale),
        out_shape=(
            jax.ShapeDtypeStruct(offsets.shape, jnp.float32),
            jax.ShapeDtypeStruct((2 * layers, GRID, GRID), jnp.float32),
            jax.ShapeDtypeStruct((2, GRID, GRID), jnp.float32),
            jax.ShapeDtypeStruct((3 * beads, 2 * slots), jnp.float32),
        ),
        in_specs=[pl.BlockSpec(memory_space=pltpu.SMEM)] + [vmem] * 8,
        out_specs=(vmem,) * 4,
        scratch_shapes=[
            pltpu.VMEM((3 * GRID, 2 * layers * GRID), jnp.bfloat16),
            pltpu.VMEM((3 * GRID, 2 * layers * GRID), jnp.bfloat16),
            pltpu.VMEM((2 * layers * GRID, group * chains), jnp.bfloat16),
            pltpu.VMEM((3 * GRID, group * chains), jnp.bfloat16),
            pltpu.VMEM((3 * GRID, 2 * layers * GRID), jnp.float32),
            pltpu.VMEM((3 * beads, chains), jnp.float32),
        ],
        compiler_params=pltpu.CompilerParams(vmem_limit_bytes=48 * 1024 * 1024),
    )(
        crossing_counts,
        cells,
        offsets,
        displacements,
        block_split.reshape(1, chains),
        square.reshape(2 * layers, GRID, GRID),
        low,
        high,
        crossing.reshape(1, 2 * slots),
    )
    grid = grid.reshape(2, layers, GRID, GRID)
    carried = shifted(carry, "dom", 1)
    grid = jnp.concatenate([grid[:, :1] + carried[:, None], grid[:, 1:]], axis=1)
    density = lax.psum_scatter(
        grid.reshape(2, layers, plane), "rep", scatter_dimension=2, tiled=True
    )
    arrived_up = shifted(picked[:, :slots].reshape(3, -1), "dom", 1)
    arrived_down = shifted(picked[:, slots:].reshape(3, -1), "dom", -1)
    return new_offsets, density, jnp.stack([arrived_up, arrived_down])


def solution(mesh):
    in_specs = (
        P(None, ("dom", "rep")),
        P(None, ("dom", "rep")),
        P(None, ("dom", "rep")),
        P(("dom", "rep")),
        P(None, "dom", None),
        P(("dom", "rep"), None, None),
        P(("dom", "rep"), None),
    )
    out_specs = (P(None, ("dom", "rep")), P(None, "dom", "rep"), P(None, None, ("dom", "rep")))
    return jax.shard_map(shards, mesh=mesh, in_specs=in_specs, out_specs=out_specs, check_vma=False)
```

time: 612 us -> 438 us (0.72)
  local copies, waits for them, and re-layouts: 295 us -> 83 us
  other arithmetic: 187 us -> 0.11 us
  waiting for transfers between devices: 107 us -> 285 us
  Pallas kernels: 0 us -> 49.7 us
    unnamed x1 -> x2, waiting for transfers between devices: 0.02 us -> 283 us
    gather x4 -> x0, local copies, waits for them, and re-layouts: 244 us -> none  [the longest x2 243 us: move_beads(): field_push = forces[:, lookup]]
    scatter-add x3 -> x0, other arithmetic: 171 us -> none  [the longest x1 171 us: deposit(): return grid_sum.at[all_index].add(all_weight)]
    psum x1 -> x0, waiting for transfers between devices: 105 us -> none  [reduce_grid(): summed_all = lax.psum(grid_sum, 'rep')]
    unnamed x43 -> x17, local copies, waits for them, and re-layouts: 5.15 us -> 79.7 us
    pallas_call x0 -> x1, Pallas kernels: none -> 49.7 us  [shards(): pl.pallas_call(functools.partial(step_kernel, layers, beads, chains, slot...]
    another operation x2 -> x1, local copies, waits for them, and re-layouts: 35.1 us -> 1.62 us  [shards(): square.reshape(2 * layers, GRID, GRID)]
  transfers between devices with their start and end apart: 6 -> 6, of which waited for: 3 -> 4; matrix products, arithmetic and copies ran while one was open for 3% -> 1% of each run, Pallas kernels for 0% -> 0%
where the time goes in v1:
time: 438 us; the launch traced here: 434 us
  waiting for transfers between devices  285 us (65%)
  local copies, waits for them, and re-layouts  83 us (19%)
  Pallas kernels  49.7 us (11%)
  between operations  14.1 us (3%)
    unnamed x2, waiting for transfers between devices  283 us
    unnamed x17, local copies, waits for them, and re-layouts  79.7 us
    pallas_call x1, Pallas kernels, shards(): pl.pallas_call(functools.partial(step_kernel, layers, beads, chains, slot...  49.7 us
  transfers between devices with their start and end apart: 6, of which 4 were waited for; matrix products, arithmetic and copies ran while one was open for 1% of the time, Pallas kernels for 0%

profile of v1, /device:TPU:15, one launch (start us, length us, event | category | flops | bytes accessed | tf_op | source)
XLA Modules:
  0.0 434.2 jit_solution(17920573599359248024)
XLA Ops:
  7.2 0.0 reduce-scatter.4.cloned.1.call-start
  7.2 1.5 copy.17
  8.7 0.6 reshape.28
  9.3 0.1 slice_bitcast_fusion.2
  9.4 0.7 collective-permute-start.1
  10.1 0.1 collective-permute-start
  10.2 1.6 reshape_reshape.3.field_ref
  11.8 0.8 reshape.29.cross_ref
  12.6 0.0 collective-permute-done.1.high_ref
  12.6 0.0 collective-permute-done.low_ref
  12.6 0.0 copy-start
  12.6 0.9 copy-done
  13.5 0.0 copy-start.1
  13.5 0.9 copy-done.1
  14.5 0.0 copy-start.2
  14.5 0.9 copy-done.2
  15.4 0.0 copy-start.3
  15.4 0.7 copy-done.3
  16.1 0.0 copy-start.4
  16.1 0.7 copy-done.4
  16.8 49.7 %shard_map.94 = (f32[3,16384]{1,0:T(4,128)}, f32[4,192,192]{2,1,0:T(8,128)S(1)}, f32[2,192,192]{2,1,0:T(8,128)S(1)}, f32[96,32]{1,0:T(8,128)S(1)}) custom-call(s32[1,2]{1,0:T(1,128)S(1)} %copy-done.4, s32[3,16384]{1,0:T(4,128)S(1)} %copy-done, f32[3,16384]{1,0:T(4,128)S(1)} %copy-done.1, f32[3,16384]{1,0:T(4,128)S(1)} %copy-done.2, s32[1,512]{1,0:T(1,128)S(1)} %bitcast.24, ...), custom_call_target="tpu_custom_call" | custom-call | tf_op jit(solution)/shard_map/pallas_call | solution.py:139
  66.5 0.5 collective-permute-start.2
  67.0 1.3 collective-permute-done.2
  68.4 0.1 fusion
  68.4 0.1 pad_maximum_fusion
  68.5 32.9 %copy.25 = f32[2,2,192,192]{1,0,3,2:T(2,128)} copy(f32[2,2,192,192]{3,2,0,1:T(8,128)S(1)} %pad_maximum_fusion) | data formatting | bytes 1179648
  101.3 35.1 %reshape.34 = f32[36864,4]{1,0:T(8,128)} reshape(f32[36864,2,2]{2,1,0:T(2,128)} %bitcast.25) | data formatting | bytes 1179648
  136.5 0.0 reduce-scatter.4.cloned.1.call-update
  136.5 0.1 fusion.1
  136.6 0.1 reshape.32
  136.7 0.1 reshape.33
  136.8 0.4 collective-permute-start.4
  137.2 0.1 collective-permute-start.3
  137.3 0.7 collective-permute-done.4
  138.0 0.3 collective-permute-done.3
  138.4 0.6 copy.21
  139.0 282.9 %reduce-scatter.4.cloned.1.call-done = f32[2304,4]{1,0:T(8,128)} async-done(((f32[36864,4]{1,0:T(8,128)}), f32[2304,4]{1,0:T(8,128)}) %reduce-scatter.4.cloned.1.call-update) | async-done | bytes 36880
  421.9 2.7 reshape.35
  424.6 2.7 copy.23
  (2 shorter events, 0.0 us)
Async XLA Ops:
  7.2 414.7 %reduce-scatter.4.cloned.1.call-start = ((), (), s32[]{:S(2)}) async-start(), calls=%async_computation.1 | async-start | bytes 20054016
  9.4 3.2 collective-permute-start.1
  10.1 2.5 collective-permute-start
  12.6 1.0 copy-start
  13.5 0.9 copy-start.1
  14.5 0.9 copy-start.2
  15.4 0.7 copy-start.3
  16.1 0.7 copy-start.4
  66.5 1.8 collective-permute-start.2
  136.8 1.3 collective-permute-start.4
  137.2 1.2 collective-permute-start.3
Sparse Core Ops, SparseCore 0:
  136.6 285.2 reduce-scatter.3

commit v2 on v1

--- a/solution.py
+++ b/solution.py
@@ -24,10 +24,10 @@
 
     for s in range(2):
         for layer in range(layers):
-            q = s * layers + layer
-            w = field_ref[q]
-            below = low_ref[s] if layer == 0 else field_ref[q - 1]
-            above = high_ref[s] if layer == layers - 1 else field_ref[q + 1]
+            p, q = s * layers + layer, layer * 2 + s
+            w = field_ref[p]
+            below = low_ref[s] if layer == 0 else field_ref[p - 1]
+            above = high_ref[s] if layer == layers - 1 else field_ref[p + 1]
             back_x = jnp.concatenate([w[GRID - 1 :], w[: GRID - 1]], axis=0)
             ahead_x = jnp.concatenate([w[1:], w[:1]], axis=0)
             back_y = jnp.concatenate([w[:, GRID - 1 :], w[:, : GRID - 1]], axis=1)
@@ -64,7 +64,7 @@
             gap_before = gap(cells_ref[:, before], offsets_ref[:, before], cell, off)
             bond = gap_after - gap_before
             species = (split_ref[...] <= j).astype(jnp.int32)
-            key = (species * layers + cell[2:3]) * GRID + cell[1:2]
+            key = (cell[2:3] * 2 + species) * GRID + cell[1:2]
             chosen = jnp.where(key_rows == key, 1.0, 0.0).astype(jnp.bfloat16)
             hot[:, jj * chains : (jj + 1) * chains] = chosen
             found = jnp.dot(table_hi[...], chosen, preferred_element_type=jnp.float32)
@@ -95,28 +95,101 @@
     upper = total[GRID : 2 * GRID] + total[2 * GRID :]
     lower = (ones - upper) * scale
     upper = upper * scale
-    for s in range(2):
-        for layer in range(layers):
-            q = s * layers + layer
-            part = lower[:, q * GRID : (q + 1) * GRID]
-            if layer > 0:
-                part = part + upper[:, (q - 1) * GRID : q * GRID]
-            grid_ref[q] = part
-        last = s * layers + layers - 1
-        carry_ref[s] = upper[:, last * GRID : (last + 1) * GRID]
+    pair = 2 * GRID
+    shares, rows = carry_ref.shape[0], carry_ref.shape[1]
+    for layer in range(layers):
+        part = lower[:, layer * pair : (layer + 1) * pair]
+        if layer > 0:
+            part = part + upper[:, (layer - 1) * pair : layer * pair]
+        for r in range(shares):
+            grid_ref[r, layer] = part[r * rows : (r + 1) * rows]
+    for r in range(shares):
+        carry_ref[r] = upper[r * rows : (r + 1) * rows, (layers - 1) * pair :]
 
     chain_rows = lax.broadcasted_iota(jnp.int32, (chains, 2 * slots), 0)
     pick = jnp.where(chain_rows == cross_ref[...], 1.0, 0.0)
     picked = jnp.dot(
         position[...], pick, precision=lax.Precision.HIGHEST, preferred_element_type=jnp.float32
     )
-    rows = lax.broadcasted_iota(jnp.int32, picked.shape, 0)
+    element = lax.broadcasted_iota(jnp.int32, picked.shape, 0)
     slot = lax.broadcasted_iota(jnp.int32, picked.shape, 1)
     upward = slot < slots
     lift = jnp.where(upward, -float(layers), float(layers))
-    picked = jnp.where(rows >= 2 * beads, picked + lift, picked)
+    picked = jnp.where(element >= 2 * beads, picked + lift, picked)
     limit = jnp.where(upward, count_ref[0, 0], slots + count_ref[0, 1])
-    picked_ref[...] = jnp.where(slot < limit, picked, 0.0)
+    picked = jnp.where(slot < limit, picked, 0.0)
+    picked_ref[0] = picked[:, :slots]
+    picked_ref[1] = picked[:, slots:]
+
+
+def exchange_kernel(
+    count, domains, layers,
+    grid_ref, carry_ref, picked_ref, density_ref, arrivals_ref,
+    base, carried, crossed, slots, side_send, side_recv, send, recv,
+):
+    rep, dom = lax.axis_index("rep"), lax.axis_index("dom")
+    above, below = lax.rem(dom + 1, domains), lax.rem(dom + domains - 1, domains)
+    mesh_id = pl.DeviceIdType.MESH
+
+    barrier = pltpu.get_barrier_semaphore()
+    for side in (above, below):
+        pl.semaphore_signal(barrier, inc=1, device_id=(side, rep), device_id_type=mesh_id)
+
+    @pl.loop(1, count)
+    def _(o):
+        target = lax.rem(rep + o, count)
+        pl.semaphore_signal(barrier, inc=1, device_id=(dom, target), device_id_type=mesh_id)
+
+    pl.semaphore_wait(barrier, count + 1)
+
+    def side_copy(source, landing, number, side):
+        return pltpu.make_async_remote_copy(
+            src_ref=source, dst_ref=landing,
+            send_sem=side_send.at[number], recv_sem=side_recv.at[number],
+            device_id=(side, rep), device_id_type=mesh_id,
+        )
+
+    carry_copy = side_copy(carry_ref, carried, 0, above)
+    up_copy = side_copy(picked_ref.at[0], crossed.at[0], 1, above)
+    down_copy = side_copy(picked_ref.at[1], crossed.at[1], 2, below)
+    carry_copy.start()
+
+    def block_copy(layer, o):
+        target = lax.rem(rep + o, count)
+        source = base.at[target] if layer == 0 else grid_ref.at[target, layer]
+        return pltpu.make_async_remote_copy(
+            src_ref=source, dst_ref=slots.at[layer, o],
+            send_sem=send.at[layer, o], recv_sem=recv.at[layer, o],
+            device_id=(dom, target), device_id_type=mesh_id,
+        )
+
+    order = list(range(1, layers)) + [0]
+    for layer in order:
+        if layer == 0:
+            carry_copy.wait()
+            base[...] = grid_ref[:, 0] + carried[...]
+
+        @pl.loop(1, count)
+        def _(o):
+            block_copy(layer, o).start()
+
+    up_copy.start()
+    down_copy.start()
+
+    for layer in order:
+        own = base[rep] if layer == 0 else grid_ref[rep, layer]
+
+        def gather_in(o, summed):
+            block_copy(layer, o).wait()
+            return summed + slots[layer, o]
+
+        summed = lax.fori_loop(1, count, gather_in, own)
+        density_ref[0, layer] = summed[:, :GRID]
+        density_ref[1, layer] = summed[:, GRID:]
+
+    up_copy.wait()
+    down_copy.wait()
+    arrivals_ref[...] = crossed[...]
 
 
 def shifted(value, axis, steps):
@@ -135,14 +208,16 @@
     square = fields.reshape(2, layers, GRID, GRID)
     low = shifted(square[:, layers - 1], "dom", 1)
     high = shifted(square[:, 0], "dom", -1)
+    count, domains = lax.axis_size("rep"), lax.axis_size("dom")
+    rows = GRID // count
     vmem = pl.BlockSpec(memory_space=pltpu.VMEM)
     new_offsets, grid, carry, picked = pl.pallas_call(
         functools.partial(step_kernel, layers, beads, chains, slots, group, scale),
         out_shape=(
             jax.ShapeDtypeStruct(offsets.shape, jnp.float32),
-            jax.ShapeDtypeStruct((2 * layers, GRID, GRID), jnp.float32),
-            jax.ShapeDtypeStruct((2, GRID, GRID), jnp.float32),
-            jax.ShapeDtypeStruct((3 * beads, 2 * slots), jnp.float32),
+            jax.ShapeDtypeStruct((count, layers, rows, 2 * GRID), jnp.float32),
+            jax.ShapeDtypeStruct((count, rows, 2 * GRID), jnp.float32),
+            jax.ShapeDtypeStruct((2, 3 * beads, slots), jnp.float32),
         ),
         in_specs=[pl.BlockSpec(memory_space=pltpu.SMEM)] + [vmem] * 8,
         out_specs=(vmem,) * 4,
@@ -166,15 +241,33 @@
         high,
         crossing.reshape(1, 2 * slots),
     )
-    grid = grid.reshape(2, layers, GRID, GRID)
-    carried = shifted(carry, "dom", 1)
-    grid = jnp.concatenate([grid[:, :1] + carried[:, None], grid[:, 1:]], axis=1)
-    density = lax.psum_scatter(
-        grid.reshape(2, layers, plane), "rep", scatter_dimension=2, tiled=True
-    )
-    arrived_up = shifted(picked[:, :slots].reshape(3, -1), "dom", 1)
-    arrived_down = shifted(picked[:, slots:].reshape(3, -1), "dom", -1)
-    return new_offsets, density, jnp.stack([arrived_up, arrived_down])
+    density, arrivals = pl.pallas_call(
+        functools.partial(exchange_kernel, count, domains, layers),
+        out_shape=(
+            jax.ShapeDtypeStruct((2, layers, rows, GRID), jnp.float32),
+            jax.ShapeDtypeStruct((2, 3 * beads, slots), jnp.float32),
+        ),
+        in_specs=[vmem] * 3,
+        out_specs=(vmem,) * 2,
+        scratch_shapes=[
+            pltpu.VMEM((count, rows, 2 * GRID), jnp.float32),
+            pltpu.VMEM((count, rows, 2 * GRID), jnp.float32),
+            pltpu.VMEM((2, 3 * beads, slots), jnp.float32),
+            pltpu.VMEM((layers, count, rows, 2 * GRID), jnp.float32),
+            pltpu.SemaphoreType.DMA((3,)),
+            pltpu.SemaphoreType.DMA((3,)),
+            pltpu.SemaphoreType.DMA((layers, count)),
+            pltpu.SemaphoreType.DMA((layers, count)),
+        ],
+        compiler_params=pltpu.CompilerParams(
+            collective_id=0, has_side_effects=True, vmem_limit_bytes=16 * 1024 * 1024
+        ),
+    )(grid, carry, picked)
+    return (
+        new_offsets,
+        density.reshape(2, layers, rows * GRID),
+        arrivals.reshape(2, 3, beads * slots),
+    )
 
 
 def solution(mesh):

time: 438 us -> 81.5 us (0.19)
  waiting for transfers between devices: 285 us -> 1.14 us
  local copies, waits for them, and re-layouts: 83 us -> 5 us
  Pallas kernels: 49.7 us -> 73.7 us
  between operations: 14.1 us -> 0.69 us
    unnamed x2 -> x0, waiting for transfers between devices: 283 us -> none
    unnamed x17 -> x16, local copies, waits for them, and re-layouts: 79.7 us -> 2.17 us
    pallas_call x0 -> x1, Pallas kernels: none -> 23.1 us  [shards(): pl.pallas_call(functools.partial(exchange_kernel, count, domains, layers)...]
  transfers between devices with their start and end apart: 6 -> 2, of which waited for: 4 -> 2; matrix products, arithmetic and copies ran while one was open for 1% -> 1% of each run, Pallas kernels for 0% -> 0%
where the time goes in v2:
time: 81.5 us; the launch traced here: 81.3 us
  Pallas kernels  73.7 us (90%)
  local copies, waits for them, and re-layouts  5 us (6%)
  waiting for transfers between devices  1.14 us (1%)
    pallas_call x1, Pallas kernels, shards(): pl.pallas_call(functools.partial(step_kernel, layers, beads, chains, slot...  50.6 us
    pallas_call x1, Pallas kernels, shards(): pl.pallas_call(functools.partial(exchange_kernel, count, domains, layers)...  23.1 us
    unnamed x16, local copies, waits for them, and re-layouts  2.17 us
  transfers between devices with their start and end apart: 2, of which 2 were waited for; matrix products, arithmetic and copies ran while one was open for 1% of the time, Pallas kernels for 0%

profile of v2, /device:TPU:15, one launch (start us, length us, event | category | flops | bytes accessed | tf_op | source)
XLA Modules:
  0.0 81.3 jit_solution(1642937619891247256)
XLA Ops:
  0.6 1.5 %copy.12 = f32[2,2,36864]{2,0,1:T(2,128)S(1)} copy(f32[2,2,36864]{2,1,0:T(2,128)} %param.11) | data formatting | bytes 1179648 | tf_op args[4]
  2.2 0.6 reshape.22
  2.7 0.0 copy-start.5
  2.7 0.8 %slice_bitcast_fusion = (f32[2,192,192]{2,1,0:T(8,128)}, f32[2,192,192]{2,1,0:T(8,128)S(1)}) fusion(f32[2,2,192,192]{3,2,0,1:T(8,128)S(1)} %reshape.22), kind=kLoop, calls=%fused_computation | loop fusion | bytes 1179648 | tf_op jit(solution)/shard_map/squeeze | solution.py:210
  3.5 0.7 collective-permute-start.1
  4.2 0.0 copy-start.6
  4.2 0.0 copy-start
  4.2 0.0 copy-start.1
  4.2 0.0 copy-start.2
  4.2 0.1 collective-permute-start
  4.3 0.0 copy-done.5
  4.3 0.6 reshape_reshape.3.field_ref
  4.9 0.0 copy-done.6
  4.9 0.0 copy-start.3
  4.9 0.1 reshape.23.cross_ref
  5.0 0.0 copy-start.4
  5.0 0.8 collective-permute-done.1.high_ref
  5.8 0.4 collective-permute-done.low_ref
  6.1 0.0 copy-done
  6.1 0.0 copy-done.1
  6.1 0.0 copy-done.2
  6.1 0.0 copy-done.3
  6.1 0.0 copy-done.4
  6.2 50.6 %shard_map.94 = (f32[3,16384]{1,0:T(4,128)}, f32[16,2,12,384]{3,2,1,0:T(8,128)S(1)}, f32[16,12,384]{2,1,0:T(8,128)S(1)}, f32[2,96,16]{2,1,0:T(8,128)S(1)}) custom-call(s32[1,2]{1,0:T(1,128)S(1)} %copy-done.4, s32[3,16384]{1,0:T(4,128)S(1)} %copy-done, f32[3,16384]{1,0:T(4,128)S(1)} %copy-done.1, f32[3,16384]{1,0:T(4,128)S(1)} %copy-done.2, ...), custom_call_target="tpu_custom_call" | custom-call | tf_op jit(solution)/shard_map/pallas_call | solution.py:214
  56.7 23.1 %shard_map.95 = (f32[2,2,12,192]{3,2,1,0:T(8,128)S(1)}, f32[2,96,16]{2,1,0:T(8,128)S(1)}) custom-call(f32[16,2,12,384]{3,2,1,0:T(8,128)S(1)} %get-tuple-element.10.grid_ref, f32[16,12,384]{2,1,0:T(8,128)S(1)} %get-tuple-element.11.carry_ref, f32[2,96,16]{2,1,0:T(8,128)S(1)} %get-tuple-element.12.picked_ref), custom_call_target="tpu_custom_call" | custom-call | tf_op jit(solution)/shard_map/pallas_call | solution.py:244
  79.9 0.7 reshape.24
  80.6 0.1 reshape.25
  80.7 0.6 copy.13
Async XLA Ops:
  2.7 1.6 %copy-start.5 = (f32[2,2,36864]{2,1,0:T(2,128)S(1)}, f32[2,2,36864]{2,1,0:T(2,128)}, u32[]{:S(2)}) copy-start(f32[2,2,36864]{2,1,0:T(2,128)} %param.11) | copy-start | bytes 1769476
  3.5 2.2 %collective-permute-start.1 = (f32[2,192,192]{2,1,0:T(8,128)}, f32[2,192,192]{2,1,0:T(8,128)S(1)}, u32[]{:S(2)}, u32[]{:S(2)}) collective-permute-start(f32[2,192,192]{2,1,0:T(8,128)} %get-tuple-element.21), channel_id=1, source_target_pairs={{0,16},{16,0},{1,17},{17,1},{2,18},{18,2},{3,19},{19,3},{4,20},{20... | collective-permute-start | bytes 884744 | tf_op jit(solution)/shard_map/ppermute | solution.py:197
  4.2 0.7 copy-start.6
  4.2 1.9 %copy-start = (s32[3,16384]{1,0:T(4,128)S(1)}, s32[3,16384]{1,0:T(4,128)}, u32[]{:S(2)}) copy-start(s32[3,16384]{1,0:T(4,128)} %cells_ref.1) | copy-start | bytes 589828
  4.2 1.9 %copy-start.1 = (f32[3,16384]{1,0:T(4,128)S(1)}, f32[3,16384]{1,0:T(4,128)}, u32[]{:S(2)}) copy-start(f32[3,16384]{1,0:T(4,128)} %offsets_ref.1) | copy-start | bytes 589828
  4.2 1.9 %copy-start.2 = (f32[3,16384]{1,0:T(4,128)S(1)}, f32[3,16384]{1,0:T(4,128)}, u32[]{:S(2)}) copy-start(f32[3,16384]{1,0:T(4,128)} %displace_ref.1) | copy-start | bytes 589828
  4.2 1.9 %collective-permute-start = (f32[2,192,192]{2,1,0:T(8,128)S(1)}, f32[2,192,192]{2,1,0:T(8,128)S(1)}, u32[]{:S(2)}, u32[]{:S(2)}) collective-permute-start(f32[2,192,192]{2,1,0:T(8,128)S(1)} %get-tuple-element.22), channel_id=1, source_target_pairs={{0,16},{16,0},{1,17},{17,1},{2,18},{18,2},{3,19},{19,3},{4,20},{20... | collective-permute-start | bytes 884744 | tf_op jit(solution)/shard_map/ppermute | solution.py:197
  4.9 1.2 %copy-start.3 = (s32[512]{0:T(512)S(1)}, s32[512]{0:T(512)}, u32[]{:S(2)}) copy-start(s32[512]{0:T(512)} %param.10) | copy-start | bytes 6148
  5.0 1.2 %copy-start.4 = (s32[1,2]{1,0:T(1,128)S(1)}, s32[1,2]{1,0:T(1,128)}, u32[]{:S(2)}) copy-start(s32[1,2]{1,0:T(1,128)} %count_ref.1) | copy-start | bytes 28

commit v3 on v2

--- a/solution.py
+++ b/solution.py
@@ -13,18 +13,21 @@
 MOBILITY = 0.1
 
 
+SPLIT_MIN, SPLIT_MAX = 8, 24
+
+
 def step_kernel(
     layers, beads, chains, slots, group, scale,
     count_ref, cells_ref, offsets_ref, displace_ref, split_ref, field_ref, low_ref, high_ref,
-    cross_ref, out_ref, grid_ref, carry_ref, picked_ref,
-    table_hi, table_lo, hot, weights, total, position,
+    cross_ref, out_ref, first_ref, second_ref, carry_ref, picked_ref,
+    table, hot, weights, total, position,
 ):
-    planes = 2 * layers
-    keys = planes * GRID
+    keys = layers * GRID
+    pair = 2 * GRID
 
     for s in range(2):
         for layer in range(layers):
-            p, q = s * layers + layer, layer * 2 + s
+            p = s * layers + layer
             w = field_ref[p]
             below = low_ref[s] if layer == 0 else field_ref[p - 1]
             above = high_ref[s] if layer == layers - 1 else field_ref[p + 1]
@@ -37,8 +40,9 @@
                 force = force * 0.5
                 top = force.astype(jnp.bfloat16)
                 rest = (force - top.astype(jnp.float32)).astype(jnp.bfloat16)
-                table_hi[k * GRID : (k + 1) * GRID, q * GRID : (q + 1) * GRID] = top
-                table_lo[k * GRID : (k + 1) * GRID, q * GRID : (q + 1) * GRID] = rest
+                here = slice(k * GRID, (k + 1) * GRID)
+                table[s, here, layer * GRID : (layer + 1) * GRID] = top
+                table[s, here, keys + layer * GRID : keys + (layer + 1) * GRID] = rest
 
     total[...] = jnp.zeros_like(total)
     key_rows = lax.broadcasted_iota(jnp.int32, (keys, chains), 0)
@@ -52,8 +56,7 @@
     def columns(j):
         return pl.ds(pl.multiple_of(j * chains, 128), chains)
 
-    @pl.loop(0, beads // group)
-    def _(g):
+    def advance(g, kinds):
         for jj in range(group):
             j = g * group + jj
             here = columns(j)
@@ -63,12 +66,20 @@
             gap_after = gap(cell, off, cells_ref[:, after], offsets_ref[:, after])
             gap_before = gap(cells_ref[:, before], offsets_ref[:, before], cell, off)
             bond = gap_after - gap_before
-            species = (split_ref[...] <= j).astype(jnp.int32)
-            key = (cell[2:3] * 2 + species) * GRID + cell[1:2]
-            chosen = jnp.where(key_rows == key, 1.0, 0.0).astype(jnp.bfloat16)
-            hot[:, jj * chains : (jj + 1) * chains] = chosen
-            found = jnp.dot(table_hi[...], chosen, preferred_element_type=jnp.float32)
-            found += jnp.dot(table_lo[...], chosen, preferred_element_type=jnp.float32)
+            key = cell[2:3] * GRID + cell[1:2]
+            if len(kinds) > 1:
+                species = (split_ref[...] <= j).astype(jnp.int32)
+            found = None
+            for at, kind in enumerate(kinds):
+                own_key = key if len(kinds) == 1 else jnp.where(species == kind, key, -1)
+                chosen = jnp.where(key_rows == own_key, 1.0, 0.0).astype(jnp.bfloat16)
+                hot[at * keys : (at + 1) * keys, jj * chains : (jj + 1) * chains] = chosen
+                product = jnp.dot(
+                    table[kind],
+                    jnp.concatenate([chosen, chosen], axis=0),
+                    preferred_element_type=jnp.float32,
+                )
+                found = product if found is None else found + product
             at_x = x_rows == cell[0:1]
             push = [
                 jnp.sum(
@@ -87,24 +98,43 @@
             weights[0:GRID, here_w] = jnp.where(at_x, 1.0, 0.0).astype(jnp.bfloat16)
             weights[GRID : 2 * GRID, here_w] = jnp.where(at_x, top, 0.0).astype(jnp.bfloat16)
             weights[2 * GRID :, here_w] = jnp.where(at_x, t - top, 0.0).astype(jnp.bfloat16)
-        total[...] += lax.dot_general(
-            weights[...], hot[...], (((1,), (1,)), ((), ())), preferred_element_type=jnp.float32
+        target = slice(kinds[0] * keys, (kinds[-1] + 1) * keys)
+        total[:, target] += lax.dot_general(
+            weights[...], hot[: len(kinds) * keys], (((1,), (1,)), ((), ())),
+            preferred_element_type=jnp.float32,
         )
+
+    head, tail = SPLIT_MIN // group, SPLIT_MAX // group
+    for begin, end, kinds in ((0, head, (0,)), (head, tail, (0, 1)), (tail, beads // group, (1,))):
+        pl.loop(begin, end)(functools.partial(advance, kinds=kinds))
 
     ones = total[0:GRID]
     upper = total[GRID : 2 * GRID] + total[2 * GRID :]
     lower = (ones - upper) * scale
     upper = upper * scale
-    pair = 2 * GRID
-    shares, rows = carry_ref.shape[0], carry_ref.shape[1]
-    for layer in range(layers):
-        part = lower[:, layer * pair : (layer + 1) * pair]
-        if layer > 0:
-            part = part + upper[:, (layer - 1) * pair : layer * pair]
-        for r in range(shares):
-            grid_ref[r, layer] = part[r * rows : (r + 1) * rows]
+
+    def both(counts, layer):
+        return jnp.concatenate(
+            [
+                counts[:, s * keys + layer * GRID : s * keys + (layer + 1) * GRID]
+                for s in range(2)
+            ],
+            axis=1,
+        )
+
+    bottom = both(lower, 0)
+    top_layer = both(lower, 1) + both(upper, 0)
+    leaving = both(upper, 1)
+    shares, main = first_ref.shape[:2]
+    spare = (second_ref.shape[1] - main) // 2
+    rows = main + spare
     for r in range(shares):
-        carry_ref[r] = upper[r * rows : (r + 1) * rows, (layers - 1) * pair :]
+        first_ref[r] = top_layer[r * rows : r * rows + main]
+        second_ref[r, :rows] = bottom[r * rows : (r + 1) * rows]
+        carry_ref[r, :rows] = leaving[r * rows : (r + 1) * rows]
+        if spare:
+            second_ref[r, rows:] = top_layer[r * rows + main : (r + 1) * rows]
+            carry_ref[r, rows:] = jnp.zeros((spare, pair), jnp.float32)
 
     chain_rows = lax.broadcasted_iota(jnp.int32, (chains, 2 * slots), 0)
     pick = jnp.where(chain_rows == cross_ref[...], 1.0, 0.0)
@@ -123,9 +153,9 @@
 
 
 def exchange_kernel(
-    count, domains, layers,
-    grid_ref, carry_ref, picked_ref, density_ref, arrivals_ref,
-    base, carried, crossed, slots, side_send, side_recv, send, recv,
+    count, domains,
+    first_ref, second_ref, carry_ref, picked_ref, density_ref, arrivals_ref,
+    base, carried, crossed, first_slots, second_slots, side_send, side_recv, send, recv,
 ):
     rep, dom = lax.axis_index("rep"), lax.axis_index("dom")
     above, below = lax.rem(dom + 1, domains), lax.rem(dom + domains - 1, domains)
@@ -154,38 +184,47 @@
     down_copy = side_copy(picked_ref.at[1], crossed.at[1], 2, below)
     carry_copy.start()
 
-    def block_copy(layer, o):
+    def block_copy(part, o):
         target = lax.rem(rep + o, count)
-        source = base.at[target] if layer == 0 else grid_ref.at[target, layer]
+        source, landing = ((first_ref, first_slots), (base, second_slots))[part]
         return pltpu.make_async_remote_copy(
-            src_ref=source, dst_ref=slots.at[layer, o],
-            send_sem=send.at[layer, o], recv_sem=recv.at[layer, o],
+            src_ref=source.at[target], dst_ref=landing.at[o],
+            send_sem=send.at[part, o], recv_sem=recv.at[part, o],
             device_id=(dom, target), device_id_type=mesh_id,
         )
 
-    order = list(range(1, layers)) + [0]
-    for layer in order:
-        if layer == 0:
-            carry_copy.wait()
-            base[...] = grid_ref[:, 0] + carried[...]
-
-        @pl.loop(1, count)
-        def _(o):
-            block_copy(layer, o).start()
+    @pl.loop(1, count)
+    def _(o):
+        block_copy(0, o).start()
+
+    carry_copy.wait()
+    base[...] = second_ref[...] + carried[...]
+
+    @pl.loop(1, count)
+    def _(o):
+        block_copy(1, o).start()
 
     up_copy.start()
     down_copy.start()
 
-    for layer in order:
-        own = base[rep] if layer == 0 else grid_ref[rep, layer]
-
-        def gather_in(o, summed):
-            block_copy(layer, o).wait()
-            return summed + slots[layer, o]
-
-        summed = lax.fori_loop(1, count, gather_in, own)
-        density_ref[0, layer] = summed[:, :GRID]
-        density_ref[1, layer] = summed[:, GRID:]
+    def first_in(o, summed):
+        block_copy(0, o).wait()
+        return summed + first_slots[o]
+
+    def second_in(o, summed):
+        block_copy(1, o).wait()
+        return summed + second_slots[o]
+
+    first = lax.fori_loop(1, count, first_in, first_ref[rep])
+    second = lax.fori_loop(1, count, second_in, base[rep])
+    main = first.shape[0]
+    rows = main + (second.shape[0] - main) // 2
+    for s in range(2):
+        lanes = slice(s * GRID, (s + 1) * GRID)
+        density_ref[s, 0] = second[:rows, lanes]
+        density_ref[s, 1, :main] = first[:, lanes]
+        if rows > main:
+            density_ref[s, 1, main:] = second[rows:, lanes]
 
     up_copy.wait()
     down_copy.wait()
@@ -210,20 +249,23 @@
     high = shifted(square[:, 0], "dom", -1)
     count, domains = lax.axis_size("rep"), lax.axis_size("dom")
     rows = GRID // count
+    spare = 4 if rows % 8 == 4 else 0
+    first_shape = (count, rows - spare, 2 * GRID)
+    second_shape = (count, rows + spare, 2 * GRID)
     vmem = pl.BlockSpec(memory_space=pltpu.VMEM)
-    new_offsets, grid, carry, picked = pl.pallas_call(
+    new_offsets, first, second, carry, picked = pl.pallas_call(
         functools.partial(step_kernel, layers, beads, chains, slots, group, scale),
         out_shape=(
             jax.ShapeDtypeStruct(offsets.shape, jnp.float32),
-            jax.ShapeDtypeStruct((count, layers, rows, 2 * GRID), jnp.float32),
-            jax.ShapeDtypeStruct((count, rows, 2 * GRID), jnp.float32),
+            jax.ShapeDtypeStruct(first_shape, jnp.float32),
+            jax.ShapeDtypeStruct(second_shape, jnp.float32),
+            jax.ShapeDtypeStruct(second_shape, jnp.float32),
             jax.ShapeDtypeStruct((2, 3 * beads, slots), jnp.float32),
         ),
         in_specs=[pl.BlockSpec(memory_space=pltpu.SMEM)] + [vmem] * 8,
-        out_specs=(vmem,) * 4,
+        out_specs=(vmem,) * 5,
         scratch_shapes=[
-            pltpu.VMEM((3 * GRID, 2 * layers * GRID), jnp.bfloat16),
-            pltpu.VMEM((3 * GRID, 2 * layers * GRID), jnp.bfloat16),
+            pltpu.VMEM((2, 3 * GRID, 2 * layers * GRID), jnp.bfloat16),
             pltpu.VMEM((2 * layers * GRID, group * chains), jnp.bfloat16),
             pltpu.VMEM((3 * GRID, group * chains), jnp.bfloat16),
             pltpu.VMEM((3 * GRID, 2 * layers * GRID), jnp.float32),
@@ -242,27 +284,28 @@
         crossing.reshape(1, 2 * slots),
     )
     density, arrivals = pl.pallas_call(
-        functools.partial(exchange_kernel, count, domains, layers),
+        functools.partial(exchange_kernel, count, domains),
         out_shape=(
             jax.ShapeDtypeStruct((2, layers, rows, GRID), jnp.float32),
             jax.ShapeDtypeStruct((2, 3 * beads, slots), jnp.float32),
         ),
-        in_specs=[vmem] * 3,
+        in_specs=[vmem] * 4,
         out_specs=(vmem,) * 2,
         scratch_shapes=[
-            pltpu.VMEM((count, rows, 2 * GRID), jnp.float32),
-            pltpu.VMEM((count, rows, 2 * GRID), jnp.float32),
+            pltpu.VMEM(second_shape, jnp.float32),
+            pltpu.VMEM(second_shape, jnp.float32),
             pltpu.VMEM((2, 3 * beads, slots), jnp.float32),
-            pltpu.VMEM((layers, count, rows, 2 * GRID), jnp.float32),
+            pltpu.VMEM(first_shape, jnp.float32),
+            pltpu.VMEM(second_shape, jnp.float32),
             pltpu.SemaphoreType.DMA((3,)),
             pltpu.SemaphoreType.DMA((3,)),
-            pltpu.SemaphoreType.DMA((layers, count)),
-            pltpu.SemaphoreType.DMA((layers, count)),
+            pltpu.SemaphoreType.DMA((2, count)),
+            pltpu.SemaphoreType.DMA((2, count)),
         ],
         compiler_params=pltpu.CompilerParams(
             collective_id=0, has_side_effects=True, vmem_limit_bytes=16 * 1024 * 1024
         ),
-    )(grid, carry, picked)
+    )(first, second, carry, picked)
     return (
         new_offsets,
         density.reshape(2, layers, rows * GRID),

time: 81.5 us -> 68.7 us (0.84)
  Pallas kernels: 73.7 us -> 60.9 us
    pallas_call x1, Pallas kernels: 50.6 us -> 42 us  [shards(): pl.pallas_call(functools.partial(step_kernel, layers, beads, chains, slot...]
    pallas_call x1, Pallas kernels: 23.1 us -> 18.9 us  [shards(): pl.pallas_call(functools.partial(exchange_kernel, count, domains), out_sh...]
where the time goes in v3:
time: 68.7 us; the launch traced here: 68.5 us
  Pallas kernels  60.9 us (89%)
  local copies, waits for them, and re-layouts  5 us (7%)
  waiting for transfers between devices  1.14 us (2%)
  starting transfers between devices  0.76 us (1%)
  between operations  0.69 us (1%)
    pallas_call x1, Pallas kernels, shards(): pl.pallas_call(functools.partial(step_kernel, layers, beads, chains, slot...  42 us
    pallas_call x1, Pallas kernels, shards(): pl.pallas_call(functools.partial(exchange_kernel, count, domains), out_sh...  18.9 us
    unnamed x16, local copies, waits for them, and re-layouts  2.17 us
  transfers between devices with their start and end apart: 2, of which 2 were waited for; matrix products, arithmetic and copies ran while one was open for 1% of the time, Pallas kernels for 0%

profile of v3, /device:TPU:15, one launch (start us, length us, event | category | flops | bytes accessed | tf_op | source)
XLA Modules:
  0.0 68.5 jit_solution(5026380082565276797)
XLA Ops:
  0.6 1.5 %copy.12 = f32[2,2,36864]{2,0,1:T(2,128)S(1)} copy(f32[2,2,36864]{2,1,0:T(2,128)} %param.11) | data formatting | bytes 1179648 | tf_op args[4]
  2.2 0.6 reshape.22
  2.7 0.0 copy-start.5
  2.7 0.8 %slice_bitcast_fusion = (f32[2,192,192]{2,1,0:T(8,128)}, f32[2,192,192]{2,1,0:T(8,128)S(1)}) fusion(f32[2,2,192,192]{3,2,0,1:T(8,128)S(1)} %reshape.22), kind=kLoop, calls=%fused_computation | loop fusion | bytes 1179648 | tf_op jit(solution)/shard_map/squeeze | solution.py:249
  3.5 0.7 collective-permute-start.1
  4.2 0.0 copy-start.6
  4.2 0.0 copy-start
  4.2 0.0 copy-start.1
  4.2 0.0 copy-start.2
  4.2 0.1 collective-permute-start
  4.3 0.0 copy-done.5
  4.3 0.6 reshape_reshape.3.field_ref
  4.9 0.0 copy-done.6
  4.9 0.0 copy-start.3
  4.9 0.1 reshape.23.cross_ref
  5.0 0.0 copy-start.4
  5.0 0.8 %collective-permute-done.1.high_ref = f32[2,192,192]{2,1,0:T(8,128)S(1)} collective-permute-done((f32[2,192,192]{2,1,0:T(8,128)}, f32[2,192,192]{2,1,0:T(8,128)S(1)}, u32[]{:S(2)}, u32[]{:S(2)}) %collective-permute-start.1) | collective-permute-done | bytes 294944 | tf_op jit(solution)/shard_map/ppermute | solution.py:236
  5.8 0.4 collective-permute-done.low_ref
  6.1 0.0 copy-done
  6.1 0.0 copy-done.1
  6.1 0.0 copy-done.2
  6.1 0.0 copy-done.3
  6.1 0.0 copy-done.4
  6.2 42.0 %shard_map.94 = (f32[3,16384]{1,0:T(4,128)}, f32[16,8,384]{2,1,0:T(8,128)S(1)}, f32[16,16,384]{2,1,0:T(8,128)S(1)}, f32[16,16,384]{2,1,0:T(8,128)S(1)}, f32[2,96,16]{2,1,0:T(8,128)S(1)}) custom-call(s32[1,2]{1,0:T(1,128)S(1)} %copy-done.4, s32[3,16384]{1,0:T(4,128)S(1)} %copy-done, f32[3,16384]{1,0:T(4,128)S(1)} %copy-done.1, f32[3,16384]{1,0:T(4,128)S(1)} %copy-done.2, ...), custom_call_target="tpu_custom_call" | custom-call | tf_op jit(solution)/shard_map/pallas_call | solution.py:256
  48.2 18.9 %shard_map.95 = (f32[2,2,12,192]{3,2,1,0:T(8,128)S(1)}, f32[2,96,16]{2,1,0:T(8,128)S(1)}) custom-call(f32[16,8,384]{2,1,0:T(8,128)S(1)} %get-tuple-element.11.first_ref, f32[16,16,384]{2,1,0:T(8,128)S(1)} %get-tuple-element.12.second_ref, f32[16,16,384]{2,1,0:T(8,128)S(1)} %get-tuple-element.13.carry_ref, f32[2,96,16]{2,1,0:T(8,128)S(1)} %get-tuple-element.14.picked_ref), custom_call_target="tpu_custom_call" | custom-call | tf_op jit(solution)/shard_map/pallas_call | solution.py:286
  67.1 0.7 %reshape.24 = f32[2,2,2304]{2,1,0:T(2,128)} reshape(f32[2,2,12,192]{3,2,1,0:T(8,128)S(1)} %get-tuple-element.15) | data formatting | bytes 73728 | tf_op jit(solution)/shard_map/reshape | solution.py:311
  67.8 0.1 reshape.25
  67.9 0.6 copy.13
Async XLA Ops:
  2.7 1.6 %copy-start.5 = (f32[2,2,36864]{2,1,0:T(2,128)S(1)}, f32[2,2,36864]{2,1,0:T(2,128)}, u32[]{:S(2)}) copy-start(f32[2,2,36864]{2,1,0:T(2,128)} %param.11) | copy-start | bytes 1769476
  3.5 2.2 %collective-permute-start.1 = (f32[2,192,192]{2,1,0:T(8,128)}, f32[2,192,192]{2,1,0:T(8,128)S(1)}, u32[]{:S(2)}, u32[]{:S(2)}) collective-permute-start(f32[2,192,192]{2,1,0:T(8,128)} %get-tuple-element.23), channel_id=1, source_target_pairs={{0,16},{16,0},{1,17},{17,1},{2,18},{18,2},{3,19},{19,3},{4,20},{20... | collective-permute-start | bytes 884744 | tf_op jit(solution)/shard_map/ppermute | solution.py:236
  4.2 0.7 copy-start.6
  4.2 1.9 %copy-start = (s32[3,16384]{1,0:T(4,128)S(1)}, s32[3,16384]{1,0:T(4,128)}, u32[]{:S(2)}) copy-start(s32[3,16384]{1,0:T(4,128)} %cells_ref.1) | copy-start | bytes 589828
  4.2 1.9 %copy-start.1 = (f32[3,16384]{1,0:T(4,128)S(1)}, f32[3,16384]{1,0:T(4,128)}, u32[]{:S(2)}) copy-start(f32[3,16384]{1,0:T(4,128)} %offsets_ref.1) | copy-start | bytes 589828
  4.2 1.9 %copy-start.2 = (f32[3,16384]{1,0:T(4,128)S(1)}, f32[3,16384]{1,0:T(4,128)}, u32[]{:S(2)}) copy-start(f32[3,16384]{1,0:T(4,128)} %displace_ref.1) | copy-start | bytes 589828
  4.2 1.9 %collective-permute-start = (f32[2,192,192]{2,1,0:T(8,128)S(1)}, f32[2,192,192]{2,1,0:T(8,128)S(1)}, u32[]{:S(2)}, u32[]{:S(2)}) collective-permute-start(f32[2,192,192]{2,1,0:T(8,128)S(1)} %get-tuple-element.24), channel_id=1, source_target_pairs={{0,16},{16,0},{1,17},{17,1},{2,18},{18,2},{3,19},{19,3},{4,20},{20... | collective-permute-start | bytes 884744 | tf_op jit(solution)/shard_map/ppermute | solution.py:236
  4.9 1.2 %copy-start.3 = (s32[512]{0:T(512)S(1)}, s32[512]{0:T(512)}, u32[]{:S(2)}) copy-start(s32[512]{0:T(512)} %param.10) | copy-start | bytes 6148
  5.0 1.2 %copy-start.4 = (s32[1,2]{1,0:T(1,128)S(1)}, s32[1,2]{1,0:T(1,128)}, u32[]{:S(2)}) copy-start(s32[1,2]{1,0:T(1,128)} %count_ref.1) | copy-start | bytes 28

commit v4 on v3

--- a/solution.py
+++ b/solution.py
@@ -17,32 +17,72 @@
 
 
 def step_kernel(
-    layers, beads, chains, slots, group, scale,
-    count_ref, cells_ref, offsets_ref, displace_ref, split_ref, field_ref, low_ref, high_ref,
-    cross_ref, out_ref, first_ref, second_ref, carry_ref, picked_ref,
-    table, hot, weights, total, position,
+    layers, beads, chains, slots, group, scale, count, domains,
+    count_ref, cells_ref, offsets_ref, displace_ref, split_ref, field_ref, cross_ref,
+    out_ref, density_ref, arrivals_ref,
+    table, hot, weights, total, position, low_ref, high_ref,
+    first_ref, second_ref, carry_ref, picked_ref,
+    base, carried, crossed, first_slots, second_slots, side_send, side_recv, send, recv,
 ):
     keys = layers * GRID
     pair = 2 * GRID
 
+    rep, dom = lax.axis_index("rep"), lax.axis_index("dom")
+    above, below = lax.rem(dom + 1, domains), lax.rem(dom + domains - 1, domains)
+    mesh_id = pl.DeviceIdType.MESH
+
+    barrier = pltpu.get_barrier_semaphore()
+    for side in (above, below):
+        pl.semaphore_signal(barrier, inc=1, device_id=(side, rep), device_id_type=mesh_id)
+
+    @pl.loop(1, count)
+    def _(o):
+        target = lax.rem(rep + o, count)
+        pl.semaphore_signal(barrier, inc=1, device_id=(dom, target), device_id_type=mesh_id)
+
+    pl.semaphore_wait(barrier, count + 1)
+
+    def side_copy(source, landing, number, side):
+        return pltpu.make_async_remote_copy(
+            src_ref=source, dst_ref=landing,
+            send_sem=side_send.at[number], recv_sem=side_recv.at[number],
+            device_id=(side, rep), device_id_type=mesh_id,
+        )
+
+    halo_copies = []
+    for s in range(2):
+        top_w, bottom_w = field_ref.at[s * layers + layers - 1], field_ref.at[s * layers]
+        halo_copies.append(side_copy(top_w, low_ref.at[s], 3 + s, above))
+        halo_copies.append(side_copy(bottom_w, high_ref.at[s], 5 + s, below))
+    for copy in halo_copies:
+        copy.start()
+
+    def tabulate(s, layer, k, force):
+        force = force * 0.5
+        top = force.astype(jnp.bfloat16)
+        rest = (force - top.astype(jnp.float32)).astype(jnp.bfloat16)
+        here = slice(k * GRID, (k + 1) * GRID)
+        table[s, here, layer * GRID : (layer + 1) * GRID] = top
+        table[s, here, keys + layer * GRID : keys + (layer + 1) * GRID] = rest
+
     for s in range(2):
         for layer in range(layers):
-            p = s * layers + layer
-            w = field_ref[p]
-            below = low_ref[s] if layer == 0 else field_ref[p - 1]
-            above = high_ref[s] if layer == layers - 1 else field_ref[p + 1]
+            w = field_ref[s * layers + layer]
             back_x = jnp.concatenate([w[GRID - 1 :], w[: GRID - 1]], axis=0)
             ahead_x = jnp.concatenate([w[1:], w[:1]], axis=0)
             back_y = jnp.concatenate([w[:, GRID - 1 :], w[:, : GRID - 1]], axis=1)
             ahead_y = jnp.concatenate([w[:, 1:], w[:, :1]], axis=1)
-            forces = (back_x - ahead_x, back_y - ahead_y, below - above)
-            for k, force in enumerate(forces):
-                force = force * 0.5
-                top = force.astype(jnp.bfloat16)
-                rest = (force - top.astype(jnp.float32)).astype(jnp.bfloat16)
-                here = slice(k * GRID, (k + 1) * GRID)
-                table[s, here, layer * GRID : (layer + 1) * GRID] = top
-                table[s, here, keys + layer * GRID : keys + (layer + 1) * GRID] = rest
+            tabulate(s, layer, 0, back_x - ahead_x)
+            tabulate(s, layer, 1, back_y - ahead_y)
+
+    for copy in halo_copies:
+        copy.wait()
+    for s in range(2):
+        for layer in range(layers):
+            p = s * layers + layer
+            below_w = low_ref[s] if layer == 0 else field_ref[p - 1]
+            above_w = high_ref[s] if layer == layers - 1 else field_ref[p + 1]
+            tabulate(s, layer, 2, below_w - above_w)
 
     total[...] = jnp.zeros_like(total)
     key_rows = lax.broadcasted_iota(jnp.int32, (keys, chains), 0)
@@ -136,6 +176,31 @@
             second_ref[r, rows:] = top_layer[r * rows + main : (r + 1) * rows]
             carry_ref[r, rows:] = jnp.zeros((spare, pair), jnp.float32)
 
+    carry_copy = side_copy(carry_ref, carried, 0, above)
+    up_copy = side_copy(picked_ref.at[0], crossed.at[0], 1, above)
+    down_copy = side_copy(picked_ref.at[1], crossed.at[1], 2, below)
+    carry_copy.start()
+
+    def block_copy(part, o):
+        target = lax.rem(rep + o, count)
+        source, landing = ((first_ref, first_slots), (base, second_slots))[part]
+        return pltpu.make_async_remote_copy(
+            src_ref=source.at[target], dst_ref=landing.at[o],
+            send_sem=send.at[part, o], recv_sem=recv.at[part, o],
+            device_id=(dom, target), device_id_type=mesh_id,
+        )
+
+    @pl.loop(1, count)
+    def _(o):
+        block_copy(0, o).start()
+
+    carry_copy.wait()
+    base[...] = second_ref[...] + carried[...]
+
+    @pl.loop(1, count)
+    def _(o):
+        block_copy(1, o).start()
+
     chain_rows = lax.broadcasted_iota(jnp.int32, (chains, 2 * slots), 0)
     pick = jnp.where(chain_rows == cross_ref[...], 1.0, 0.0)
     picked = jnp.dot(
@@ -151,59 +216,6 @@
     picked_ref[0] = picked[:, :slots]
     picked_ref[1] = picked[:, slots:]
 
-
-def exchange_kernel(
-    count, domains,
-    first_ref, second_ref, carry_ref, picked_ref, density_ref, arrivals_ref,
-    base, carried, crossed, first_slots, second_slots, side_send, side_recv, send, recv,
-):
-    rep, dom = lax.axis_index("rep"), lax.axis_index("dom")
-    above, below = lax.rem(dom + 1, domains), lax.rem(dom + domains - 1, domains)
-    mesh_id = pl.DeviceIdType.MESH
-
-    barrier = pltpu.get_barrier_semaphore()
-    for side in (above, below):
-        pl.semaphore_signal(barrier, inc=1, device_id=(side, rep), device_id_type=mesh_id)
-
-    @pl.loop(1, count)
-    def _(o):
-        target = lax.rem(rep + o, count)
-        pl.semaphore_signal(barrier, inc=1, device_id=(dom, target), device_id_type=mesh_id)
-
-    pl.semaphore_wait(barrier, count + 1)
-
-    def side_copy(source, landing, number, side):
-        return pltpu.make_async_remote_copy(
-            src_ref=source, dst_ref=landing,
-            send_sem=side_send.at[number], recv_sem=side_recv.at[number],
-            device_id=(side, rep), device_id_type=mesh_id,
-        )
-
-    carry_copy = side_copy(carry_ref, carried, 0, above)
-    up_copy = side_copy(picked_ref.at[0], crossed.at[0], 1, above)
-    down_copy = side_copy(picked_ref.at[1], crossed.at[1], 2, below)
-    carry_copy.start()
-
-    def block_copy(part, o):
-        target = lax.rem(rep + o, count)
-        source, landing = ((first_ref, first_slots), (base, second_slots))[part]
-        return pltpu.make_async_remote_copy(
-            src_ref=source.at[target], dst_ref=landing.at[o],
-            send_sem=send.at[part, o], recv_sem=recv.at[part, o],
-            device_id=(dom, target), device_id_type=mesh_id,
-        )
-
-    @pl.loop(1, count)
-    def _(o):
-        block_copy(0, o).start()
-
-    carry_copy.wait()
-    base[...] = second_ref[...] + carried[...]
-
-    @pl.loop(1, count)
-    def _(o):
-        block_copy(1, o).start()
-
     up_copy.start()
     down_copy.start()
 
@@ -231,11 +243,6 @@
     arrivals_ref[...] = crossed[...]
 
 
-def shifted(value, axis, steps):
-    count = lax.axis_size(axis)
-    return lax.ppermute(value, axis, [(i, (i + steps) % count) for i in range(count)])
-
-
 def shards(cells, offsets, displacements, block_split, fields, crossing, crossing_counts):
     chains = block_split.shape[0]
     beads = cells.shape[1] // chains
@@ -245,33 +252,48 @@
     group = 4
     scale = plane * layers / (lax.axis_size("rep") * chains * beads)
     square = fields.reshape(2, layers, GRID, GRID)
-    low = shifted(square[:, layers - 1], "dom", 1)
-    high = shifted(square[:, 0], "dom", -1)
     count, domains = lax.axis_size("rep"), lax.axis_size("dom")
     rows = GRID // count
     spare = 4 if rows % 8 == 4 else 0
     first_shape = (count, rows - spare, 2 * GRID)
     second_shape = (count, rows + spare, 2 * GRID)
     vmem = pl.BlockSpec(memory_space=pltpu.VMEM)
-    new_offsets, first, second, carry, picked = pl.pallas_call(
-        functools.partial(step_kernel, layers, beads, chains, slots, group, scale),
+    new_offsets, density, arrivals = pl.pallas_call(
+        functools.partial(
+            step_kernel, layers, beads, chains, slots, group, scale, count, domains
+        ),
         out_shape=(
             jax.ShapeDtypeStruct(offsets.shape, jnp.float32),
-            jax.ShapeDtypeStruct(first_shape, jnp.float32),
-            jax.ShapeDtypeStruct(second_shape, jnp.float32),
-            jax.ShapeDtypeStruct(second_shape, jnp.float32),
+            jax.ShapeDtypeStruct((2, layers, rows, GRID), jnp.float32),
             jax.ShapeDtypeStruct((2, 3 * beads, slots), jnp.float32),
         ),
-        in_specs=[pl.BlockSpec(memory_space=pltpu.SMEM)] + [vmem] * 8,
-        out_specs=(vmem,) * 5,
+        in_specs=[pl.BlockSpec(memory_space=pltpu.SMEM)] + [vmem] * 6,
+        out_specs=(vmem,) * 3,
         scratch_shapes=[
             pltpu.VMEM((2, 3 * GRID, 2 * layers * GRID), jnp.bfloat16),
             pltpu.VMEM((2 * layers * GRID, group * chains), jnp.bfloat16),
             pltpu.VMEM((3 * GRID, group * chains), jnp.bfloat16),
             pltpu.VMEM((3 * GRID, 2 * layers * GRID), jnp.float32),
             pltpu.VMEM((3 * beads, chains), jnp.float32),
+            pltpu.VMEM((2, GRID, GRID), jnp.float32),
+            pltpu.VMEM((2, GRID, GRID), jnp.float32),
+            pltpu.VMEM(first_shape, jnp.float32),
+            pltpu.VMEM(second_shape, jnp.float32),
+            pltpu.VMEM(second_shape, jnp.float32),
+            pltpu.VMEM((2, 3 * beads, slots), jnp.float32),
+            pltpu.VMEM(second_shape, jnp.float32),
+            pltpu.VMEM(second_shape, jnp.float32),
+            pltpu.VMEM((2, 3 * beads, slots), jnp.float32),
+            pltpu.VMEM(first_shape, jnp.float32),
+            pltpu.VMEM(second_shape, jnp.float32),
+            pltpu.SemaphoreType.DMA((7,)),
+            pltpu.SemaphoreType.DMA((7,)),
+            pltpu.SemaphoreType.DMA((2, count)),
+            pltpu.SemaphoreType.DMA((2, count)),
         ],
-        compiler_params=pltpu.CompilerParams(vmem_limit_bytes=48 * 1024 * 1024),
+        compiler_params=pltpu.CompilerParams(
+            collective_id=0, has_side_effects=True, vmem_limit_bytes=48 * 1024 * 1024
+        ),
     )(
         crossing_counts,
         cells,
@@ -279,33 +301,8 @@
         displacements,
         block_split.reshape(1, chains),
         square.reshape(2 * layers, GRID, GRID),
-        low,
-        high,
         crossing.reshape(1, 2 * slots),
     )
-    density, arrivals = pl.pallas_call(
-        functools.partial(exchange_kernel, count, domains),
-        out_shape=(
-            jax.ShapeDtypeStruct((2, layers, rows, GRID), jnp.float32),
-            jax.ShapeDtypeStruct((2, 3 * beads, slots), jnp.float32),
-        ),
-        in_specs=[vmem] * 4,
-        out_specs=(vmem,) * 2,
-        scratch_shapes=[
-            pltpu.VMEM(second_shape, jnp.float32),
-            pltpu.VMEM(second_shape, jnp.float32),
-            pltpu.VMEM((2, 3 * beads, slots), jnp.float32),
-            pltpu.VMEM(first_shape, jnp.float32),
-            pltpu.VMEM(second_shape, jnp.float32),
-            pltpu.SemaphoreType.DMA((3,)),
-            pltpu.SemaphoreType.DMA((3,)),
-            pltpu.SemaphoreType.DMA((2, count)),
-            pltpu.SemaphoreType.DMA((2, count)),
-        ],
-        compiler_params=pltpu.CompilerParams(
-            collective_id=0, has_side_effects=True, vmem_limit_bytes=16 * 1024 * 1024
-        ),
-    )(first, second, carry, picked)
     return (
         new_offsets,
         density.reshape(2, layers, rows * GRID),

time: 68.7 us -> 67.7 us (0.985)
  Pallas kernels: 60.9 us -> 62.3 us
  waiting for transfers between devices: 1.14 us -> 0 us
  starting transfers between devices: 0.76 us -> 0 us
    pallas_call x1, Pallas kernels: 42 us -> 62.3 us  [shards(): pl.pallas_call(functools.partial(step_kernel, layers, beads, chains, slot...]
    pallas_call x1 -> x0, Pallas kernels: 18.9 us -> none  [shards(): pl.pallas_call(functools.partial(exchange_kernel, count, domains), out_sh...]
    ppermute x2 -> x0, waiting for transfers between devices: 1.14 us -> none  [shifted(): lax.ppermute(value, axis, [(i, (i + steps) % count) for i in range(count)])]
    another operation x1, local copies, waits for them, and re-layouts: 0.55 us -> 1.69 us  [shards(): square.reshape(2 * layers, GRID, GRID)]
    squeeze x1 -> x0, local copies, waits for them, and re-layouts: 0.81 us -> none  [shards(): high = shifted(square[:, 0], 'dom', -1)]
    ppermute x2 -> x0, starting transfers between devices: 0.76 us -> none  [shifted(): lax.ppermute(value, axis, [(i, (i + steps) % count) for i in range(count)])]
    unnamed x16 -> x14, local copies, waits for them, and re-layouts: 2.17 us -> 2 us
  transfers between devices with their start and end apart: 2 -> 0, of which waited for: 2 -> 0; matrix products, arithmetic and copies ran while one was open for 1% -> 0% of each run, Pallas kernels for 0% -> 0%
where the time goes in v4:
time: 67.7 us; the launch traced here: 67.6 us
  Pallas kernels  62.3 us (92%)
  local copies, waits for them, and re-layouts  4.6 us (7%)
  between operations  0.71 us (1%)
    pallas_call x1, Pallas kernels, shards(): pl.pallas_call(functools.partial(step_kernel, layers, beads, chains, slot...  62.3 us
    unnamed x14, local copies, waits for them, and re-layouts  2 us
    another operation x1, local copies, waits for them, and re-layouts, shards(): square.reshape(2 * layers, GRID, GRID)  1.69 us

profile of v4, /device:TPU:15, one launch (start us, length us, event | category | flops | bytes accessed | tf_op | source)
XLA Modules:
  0.0 67.6 jit_solution(10878650615487165681)
XLA Ops:
  0.6 0.0 copy-start.5
  0.6 0.7 copy-done.5
  1.3 0.1 reshape.19.cross_ref
  1.4 0.0 copy-start
  1.4 0.0 copy-start.1
  1.4 0.0 copy-start.2
  1.4 0.0 copy-start.3
  1.4 0.0 copy-start.4
  1.4 1.7 %reshape_reshape.3.field_ref = f32[4,192,192]{2,1,0:T(8,128)S(1)} reshape(f32[2,2,36864]{2,1,0:T(2,128)} %param.11) | data formatting | bytes 1179648 | tf_op jit(solution)/shard_map/reshape;reshape | solution.py:303
  3.1 0.0 copy-done
  3.1 0.0 copy-done.1
  3.1 0.0 copy-done.2
  3.1 0.0 copy-done.3
  3.2 0.0 copy-done.4
  3.2 62.3 %shard_map.94 = (f32[3,16384]{1,0:T(4,128)S(1)}, f32[2,2,12,192]{3,2,1,0:T(8,128)S(1)}, f32[2,96,16]{2,1,0:T(8,128)S(1)}) custom-call(s32[1,2]{1,0:T(1,128)S(1)} %copy-done.4, s32[3,16384]{1,0:T(4,128)S(1)} %copy-done, f32[3,16384]{1,0:T(4,128)S(1)} %copy-done.1, f32[3,16384]{1,0:T(4,128)S(1)} %copy-done.2, s32[1,512]{1,0:T(1,128)S(1)} %bitcast.1, ...), custom_call_target="tpu_custom_call" | custom-call | tf_op jit(solution)/shard_map/pallas_call | solution.py:261
  65.5 0.1 reshape.21
  65.6 0.6 copy.11
  66.2 0.7 %reshape.20 = f32[2,2,2304]{2,1,0:T(2,128)} reshape(f32[2,2,12,192]{3,2,1,0:T(8,128)S(1)} %get-tuple-element.7) | data formatting | bytes 73728 | tf_op jit(solution)/shard_map/reshape | solution.py:308
  66.9 0.7 %copy.13 = f32[3,16384]{1,0:T(4,128)} copy(f32[3,16384]{1,0:T(4,128)S(1)} %get-tuple-element.18) | data formatting | bytes 393216
Async XLA Ops:
  0.6 0.7 %copy-start.5 = (s32[1,2,16]{2,1,0:T(2,128)S(1)}, s32[1,2,16]{2,1,0:T(2,128)}, u32[]{:S(2)}) copy-start(s32[1,2,16]{2,1,0:T(2,128)} %param.12) | copy-start | bytes 388
  1.4 1.7 %copy-start = (s32[3,16384]{1,0:T(4,128)S(1)}, s32[3,16384]{1,0:T(4,128)}, u32[]{:S(2)}) copy-start(s32[3,16384]{1,0:T(4,128)} %cells_ref.1) | copy-start | bytes 589828
  1.4 1.7 %copy-start.1 = (f32[3,16384]{1,0:T(4,128)S(1)}, f32[3,16384]{1,0:T(4,128)}, u32[]{:S(2)}) copy-start(f32[3,16384]{1,0:T(4,128)} %offsets_ref.1) | copy-start | bytes 589828
  1.4 1.7 %copy-start.2 = (f32[3,16384]{1,0:T(4,128)S(1)}, f32[3,16384]{1,0:T(4,128)}, u32[]{:S(2)}) copy-start(f32[3,16384]{1,0:T(4,128)} %displace_ref.1) | copy-start | bytes 589828
  1.4 1.7 %copy-start.3 = (s32[512]{0:T(512)S(1)}, s32[512]{0:T(512)}, u32[]{:S(2)}) copy-start(s32[512]{0:T(512)} %param.10) | copy-start | bytes 6148
  1.4 1.8 %copy-start.4 = (s32[1,2]{1,0:T(1,128)S(1)}, s32[1,2]{1,0:T(1,128)}, u32[]{:S(2)}) copy-start(s32[1,2]{1,0:T(1,128)} %count_ref.1) | copy-start | bytes 28

commit v5 on v4

--- a/solution.py
+++ b/solution.py
@@ -40,23 +40,6 @@
         target = lax.rem(rep + o, count)
         pl.semaphore_signal(barrier, inc=1, device_id=(dom, target), device_id_type=mesh_id)
 
-    pl.semaphore_wait(barrier, count + 1)
-
-    def side_copy(source, landing, number, side):
-        return pltpu.make_async_remote_copy(
-            src_ref=source, dst_ref=landing,
-            send_sem=side_send.at[number], recv_sem=side_recv.at[number],
-            device_id=(side, rep), device_id_type=mesh_id,
-        )
-
-    halo_copies = []
-    for s in range(2):
-        top_w, bottom_w = field_ref.at[s * layers + layers - 1], field_ref.at[s * layers]
-        halo_copies.append(side_copy(top_w, low_ref.at[s], 3 + s, above))
-        halo_copies.append(side_copy(bottom_w, high_ref.at[s], 5 + s, below))
-    for copy in halo_copies:
-        copy.start()
-
     def tabulate(s, layer, k, force):
         force = force * 0.5
         top = force.astype(jnp.bfloat16)
@@ -65,14 +48,36 @@
         table[s, here, layer * GRID : (layer + 1) * GRID] = top
         table[s, here, keys + layer * GRID : keys + (layer + 1) * GRID] = rest
 
+    total[...] = jnp.zeros_like(total)
     for s in range(2):
         for layer in range(layers):
             w = field_ref[s * layers + layer]
             back_x = jnp.concatenate([w[GRID - 1 :], w[: GRID - 1]], axis=0)
             ahead_x = jnp.concatenate([w[1:], w[:1]], axis=0)
+            tabulate(s, layer, 0, back_x - ahead_x)
+
+    pl.semaphore_wait(barrier, count + 1)
+
+    def side_copy(source, landing, number, side):
+        return pltpu.make_async_remote_copy(
+            src_ref=source, dst_ref=landing,
+            send_sem=side_send.at[number], recv_sem=side_recv.at[number],
+            device_id=(side, rep), device_id_type=mesh_id,
+        )
+
+    halo_copies = []
+    for s in range(2):
+        top_w, bottom_w = field_ref.at[s * layers + layers - 1], field_ref.at[s * layers]
+        halo_copies.append(side_copy(top_w, low_ref.at[s], 3 + s, above))
+        halo_copies.append(side_copy(bottom_w, high_ref.at[s], 5 + s, below))
+    for copy in halo_copies:
+        copy.start()
+
+    for s in range(2):
+        for layer in range(layers):
+            w = field_ref[s * layers + layer]
             back_y = jnp.concatenate([w[:, GRID - 1 :], w[:, : GRID - 1]], axis=1)
             ahead_y = jnp.concatenate([w[:, 1:], w[:, :1]], axis=1)
-            tabulate(s, layer, 0, back_x - ahead_x)
             tabulate(s, layer, 1, back_y - ahead_y)
 
     for copy in halo_copies:
@@ -84,7 +89,6 @@
             above_w = high_ref[s] if layer == layers - 1 else field_ref[p + 1]
             tabulate(s, layer, 2, below_w - above_w)
 
-    total[...] = jnp.zeros_like(total)
     key_rows = lax.broadcasted_iota(jnp.int32, (keys, chains), 0)
     x_rows = lax.broadcasted_iota(jnp.int32, (GRID, chains), 0)
 

time: 67.7 us -> 67.9 us (level)
  no operation moved by 1% of the time
where the time goes in v5:
time: 67.9 us; the launch traced here: 67.7 us
  Pallas kernels  62.4 us (92%)
  local copies, waits for them, and re-layouts  4.6 us (7%)
  between operations  0.71 us (1%)
    pallas_call x1, Pallas kernels, shards(): pl.pallas_call(functools.partial(step_kernel, layers, beads, chains, slot...  62.4 us
    unnamed x14, local copies, waits for them, and re-layouts  2 us
    another operation x1, local copies, waits for them, and re-layouts, shards(): square.reshape(2 * layers, GRID, GRID)  1.69 us

profile of v5, /device:TPU:15, one launch (start us, length us, event | category | flops | bytes accessed | tf_op | source)
XLA Modules:
  0.0 67.7 jit_solution(15877832361172615312)
XLA Ops:
  0.6 0.0 copy-start.5
  0.6 0.7 copy-done.5
  1.3 0.1 reshape.19.cross_ref
  1.4 0.0 copy-start
  1.4 0.0 copy-start.1
  1.4 0.0 copy-start.2
  1.4 0.0 copy-start.3
  1.4 0.0 copy-start.4
  1.4 1.7 %reshape_reshape.3.field_ref = f32[4,192,192]{2,1,0:T(8,128)S(1)} reshape(f32[2,2,36864]{2,1,0:T(2,128)} %param.11) | data formatting | bytes 1179648 | tf_op jit(solution)/shard_map/reshape;reshape | solution.py:307
  3.1 0.0 copy-done
  3.1 0.0 copy-done.1
  3.1 0.0 copy-done.2
  3.1 0.0 copy-done.3
  3.2 0.0 copy-done.4
  3.2 62.4 %shard_map.94 = (f32[3,16384]{1,0:T(4,128)S(1)}, f32[2,2,12,192]{3,2,1,0:T(8,128)S(1)}, f32[2,96,16]{2,1,0:T(8,128)S(1)}) custom-call(s32[1,2]{1,0:T(1,128)S(1)} %copy-done.4, s32[3,16384]{1,0:T(4,128)S(1)} %copy-done, f32[3,16384]{1,0:T(4,128)S(1)} %copy-done.1, f32[3,16384]{1,0:T(4,128)S(1)} %copy-done.2, s32[1,512]{1,0:T(1,128)S(1)} %bitcast.1, ...), custom_call_target="tpu_custom_call" | custom-call | tf_op jit(solution)/shard_map/pallas_call | solution.py:265
  65.6 0.1 reshape.21
  65.7 0.6 copy.11
  66.3 0.7 %reshape.20 = f32[2,2,2304]{2,1,0:T(2,128)} reshape(f32[2,2,12,192]{3,2,1,0:T(8,128)S(1)} %get-tuple-element.7) | data formatting | bytes 73728 | tf_op jit(solution)/shard_map/reshape | solution.py:312
  67.0 0.7 %copy.13 = f32[3,16384]{1,0:T(4,128)} copy(f32[3,16384]{1,0:T(4,128)S(1)} %get-tuple-element.18) | data formatting | bytes 393216
Async XLA Ops:
  0.6 0.7 %copy-start.5 = (s32[1,2,16]{2,1,0:T(2,128)S(1)}, s32[1,2,16]{2,1,0:T(2,128)}, u32[]{:S(2)}) copy-start(s32[1,2,16]{2,1,0:T(2,128)} %param.12) | copy-start | bytes 388
  1.4 1.7 %copy-start = (s32[3,16384]{1,0:T(4,128)S(1)}, s32[3,16384]{1,0:T(4,128)}, u32[]{:S(2)}) copy-start(s32[3,16384]{1,0:T(4,128)} %cells_ref.1) | copy-start | bytes 589828
  1.4 1.7 %copy-start.1 = (f32[3,16384]{1,0:T(4,128)S(1)}, f32[3,16384]{1,0:T(4,128)}, u32[]{:S(2)}) copy-start(f32[3,16384]{1,0:T(4,128)} %offsets_ref.1) | copy-start | bytes 589828
  1.4 1.7 %copy-start.2 = (f32[3,16384]{1,0:T(4,128)S(1)}, f32[3,16384]{1,0:T(4,128)}, u32[]{:S(2)}) copy-start(f32[3,16384]{1,0:T(4,128)} %displace_ref.1) | copy-start | bytes 589828
  1.4 1.7 %copy-start.3 = (s32[512]{0:T(512)S(1)}, s32[512]{0:T(512)}, u32[]{:S(2)}) copy-start(s32[512]{0:T(512)} %param.10) | copy-start | bytes 6148
  1.4 1.8 %copy-start.4 = (s32[1,2]{1,0:T(1,128)S(1)}, s32[1,2]{1,0:T(1,128)}, u32[]{:S(2)}) copy-start(s32[1,2]{1,0:T(1,128)} %count_ref.1) | copy-start | bytes 28
